TPU v7x, 32 devices: a whole 2x2x4 slice. The times are simulated.
32 devices in a mesh: seq: 8 (over z, x), dp: 4 (over y, core).
Axes of the slice: x: 2, y: 2, z: 4, core: 2. Of those that a mesh axis runs over, the one named last changes fastest.
Arguments:
- layer_input: bfloat16 [16384, 576], P(('seq', 'dp')), may hold values from -6 to 6
- w_qkv: bfloat16 [552960], P(('seq', 'dp')), may hold values from -0.25 to 0.25
- w_out: bfloat16 [331776], P(('seq', 'dp')), may hold values from -4 to 4
- w_gu: bfloat16 [1769472], P(('seq', 'dp')), may hold values from -0.25 to 0.25
- w_down: bfloat16 [884736], P(('seq', 'dp')), may hold values from -0.15625 to 0.15625
- norm_gains: float32 [2, 576], replicated, may hold values from 0.1 to 1.9
- lengths: int32 [4, 6], P('dp'), may hold values from 1 to 2048, 4096 in all within a row
- cotangent: bfloat16 [16384, 576], P(('seq', 'dp')), may hold values from -6 to 6
Outputs:
- layer_output: bfloat16 [16384, 576], P(('seq', 'dp'))
- input_grad: float32 [16384, 576], P(('seq', 'dp'))
- g_qkv: float32 [552960], P(('seq', 'dp'))
- g_out: float32 [331776], P(('seq', 'dp'))
- g_gu: float32 [1769472], P(('seq', 'dp'))
- g_down: float32 [884736], P(('seq', 'dp'))
- gains_grad: float32 [2, 576], replicated
Inputs may be any that keep to these rules, and one draw needn't show every extreme that they name: Each row lists the lengths of the 6 sequences of one dp group in order; a row sums to 4096, and its largest entry is exactly 2048.
All inputs are finite; a program needn't handle non-finite values.
Results may differ from a plain program's by a relative error of at most 0.012.
Values may be sent and summed in bfloat16 or wider, within the bound.
A program may use at most 128 MiB of HBM per device.

v0:
```python
import math
import jax
import jax.numpy as jnp
from jax import lax
from jax.sharding import PartitionSpec as P

D = 576
QUERY_HEADS = 9
KEY_VALUE_HEADS = 3
HEAD_SIZE = 64
FF = 1536
EPS = 1e-05
THETA = 100000.0
MASKED = -1e30


def rms_norm(value_rows, gain):
    return (
        value_rows
        * lax.rsqrt(jnp.mean(value_rows * value_rows, axis=-1, keepdims=True) + EPS)
        * gain
    )


def apply_rotary(value_rows, token_position):
    half = value_rows.shape[-1] // 2
    freq = jnp.exp(
        jnp.arange(half, dtype=jnp.float32) * (-2.0 * math.log(THETA) / value_rows.shape[-1])
    )
    angle = token_position.astype(jnp.float32)[:, None] * freq[None, :]
    cosine = jnp.cos(angle)[:, None, :]
    sine = jnp.sin(angle)[:, None, :]
    first = value_rows[..., :half]
    second = value_rows[..., half:]
    return jnp.concatenate(
        [first * cosine - second * sine, second * cosine + first * sine], axis=-1
    )


def layout(lengths_row, index):
    ends = jnp.cumsum(lengths_row, dtype=jnp.int32)
    done = ends[None, :] <= index[:, None]
    segment_index = jnp.sum(done.astype(jnp.int32), axis=1, dtype=jnp.int32)
    token_position = index - jnp.sum(
        jnp.where(done, lengths_row[None, :], 0), axis=1, dtype=jnp.int32
    )
    return (segment_index, token_position)


def silu_product(gate_up):
    width = gate_up.shape[1] // 2
    return jax.nn.silu(gate_up[:, :width]) * gate_up[:, width:]


def per_device(layer_input, w_qkv, w_out, w_gu, w_down, norm_gains, lengths, cotangent):
    token_rows = layer_input.shape[0]
    seq_count = lax.axis_size("seq")
    group = token_rows * seq_count
    heads_per_group = QUERY_HEADS // KEY_VALUE_HEADS
    query_width = QUERY_HEADS * HEAD_SIZE
    key_width = KEY_VALUE_HEADS * HEAD_SIZE
    scale = 1.0 / math.sqrt(HEAD_SIZE)
    block_current = math.gcd(group, 512)
    blocks = group // block_current
    numbers = jnp.arange(blocks, dtype=jnp.int32)

    def fetch_weights():
        parts = (
            lax.all_gather(w_qkv, ("seq", "dp"), axis=0, tiled=True),
            lax.all_gather(w_out, ("seq", "dp"), axis=0, tiled=True),
            lax.all_gather(w_gu, ("seq", "dp"), axis=0, tiled=True),
            lax.all_gather(w_down, ("seq", "dp"), axis=0, tiled=True),
        )
        return (
            parts[0].reshape(D, -1),
            parts[1].reshape(query_width, D),
            parts[2].reshape(D, 2 * FF),
            parts[3].reshape(FF, D),
        )

    def fetch_pairs(keys_mine, values_mine):
        return (
            lax.all_gather(keys_mine, "seq", axis=0, tiled=True),
            lax.all_gather(values_mine, "seq", axis=0, tiled=True),
        )

    lengths_row = lengths[0]
    query_index = lax.axis_index("seq") * token_rows + jnp.arange(token_rows, dtype=jnp.int32)
    query_segment, query_token_position = layout(lengths_row, query_index)
    key_index = jnp.arange(group, dtype=jnp.int32)
    key_valid = key_index >= 0
    key_segment = layout(lengths_row, jnp.maximum(key_index, 0))[0]

    def block_parts(key_value_pairs, number):
        start_offset = number * block_current
        key_window_part = lax.dynamic_slice_in_dim(
            key_value_pairs[0], start_offset, block_current, 0
        ).reshape(block_current, KEY_VALUE_HEADS, HEAD_SIZE)
        value_window_part = lax.dynamic_slice_in_dim(
            key_value_pairs[1], start_offset, block_current, 0
        ).reshape(block_current, KEY_VALUE_HEADS, HEAD_SIZE)
        seg_slice = lax.dynamic_slice_in_dim(key_segment, start_offset, block_current, 0)
        idx_slice = lax.dynamic_slice_in_dim(key_index, start_offset, block_current, 0)
        valid_slice = lax.dynamic_slice_in_dim(key_valid, start_offset, block_current, 0)
        allowed = (
            valid_slice[None, :]
            & (query_segment[:, None] == seg_slice[None, :])
            & (query_index[:, None] >= idx_slice[None, :])
        )
        return (key_window_part, value_window_part, allowed[None, None])

    mixing_in, mixing_out, expand_matrix, shrink_matrix = fetch_weights()
    inputs = layer_input.astype(jnp.float32)
    normed, norm_back = jax.vjp(rms_norm, inputs, norm_gains[0])
    normed_low = normed.astype(jnp.bfloat16)
    projected_output = jnp.dot(normed_low, mixing_in, preferred_element_type=jnp.float32)
    rotated_query, query_unrot = jax.vjp(
        lambda part: apply_rotary(
            part.reshape(token_rows, QUERY_HEADS, HEAD_SIZE), query_token_position
        ),
        projected_output[:, :query_width],
    )
    keys_rot, unrotated_keys = jax.vjp(
        lambda part: apply_rotary(
            part.reshape(token_rows, KEY_VALUE_HEADS, HEAD_SIZE), query_token_position
        ),
        projected_output[:, query_width : query_width + key_width],
    )
    query_lower_precision = rotated_query.astype(jnp.bfloat16).reshape(
        token_rows, KEY_VALUE_HEADS, heads_per_group, HEAD_SIZE
    )
    keys_low = keys_rot.astype(jnp.bfloat16).reshape(token_rows, key_width)
    values_low = projected_output[:, query_width + key_width :].astype(jnp.bfloat16)
    pairs_now = fetch_pairs(keys_low, values_low)

    def scores_of(key_window_part, allowed):
        raw = (
            jnp.einsum(
                "tkgd,skd->kgts",
                query_lower_precision,
                key_window_part,
                preferred_element_type=jnp.float32,
            )
            * scale
        )
        return jnp.where(allowed, raw, MASKED)

    statistic_dims = (KEY_VALUE_HEADS, heads_per_group, token_rows)

    def stat_step(carry, number):
        key_window_part, value_window_part, allowed = block_parts(pairs_now, number)
        scores = scores_of(key_window_part, allowed)
        highest = jnp.maximum(carry[0], jnp.max(scores, axis=-1))
        summed = carry[1] * jnp.exp(carry[0] - highest) + jnp.sum(
            jnp.where(allowed, jnp.exp(scores - highest[..., None]), 0.0), axis=-1
        )
        return ((highest, summed), None)

    stats = lax.scan(
        stat_step,
        (jnp.full(statistic_dims, MASKED, jnp.float32), jnp.zeros(statistic_dims, jnp.float32)),
        numbers,
    )[0]
    log_total = stats[0] + jnp.log(stats[1])

    def probs_of(key_value_pairs, number):
        key_window_part, value_window_part, allowed = block_parts(key_value_pairs, number)
        scores = scores_of(key_window_part, allowed)
        probs = jnp.where(allowed, jnp.exp(scores - log_total[..., None]), 0.0)
        return (key_window_part, value_window_part, probs)

    def out_step(summed, number):
        key_window_part, value_window_part, probs = probs_of(pairs_now, number)
        return (
            summed
            + jnp.einsum(
                "kgts,skd->tkgd",
                probs.astype(jnp.bfloat16),
                value_window_part,
                preferred_element_type=jnp.float32,
            ),
            None,
        )

    head_layout_dims = (token_rows, KEY_VALUE_HEADS, heads_per_group, HEAD_SIZE)
    attended_rows = lax.scan(out_step, jnp.zeros(head_layout_dims, jnp.float32), numbers)[0]
    attended_low = attended_rows.reshape(token_rows, query_width).astype(jnp.bfloat16)
    mid = inputs + jnp.dot(attended_low, mixing_out, preferred_element_type=jnp.float32)
    normed_two, norm_two_back = jax.vjp(rms_norm, mid, norm_gains[1])
    normed_two_low = normed_two.astype(jnp.bfloat16)
    gate_up = jnp.dot(normed_two_low, expand_matrix, preferred_element_type=jnp.float32)
    hidden, hidden_back = jax.vjp(silu_product, gate_up)
    hidden_low = hidden.astype(jnp.bfloat16)
    result = (mid + jnp.dot(hidden_low, shrink_matrix, preferred_element_type=jnp.float32)).astype(
        jnp.bfloat16
    )
    mixing_in, mixing_out, expand_matrix, shrink_matrix = fetch_weights()
    pairs_back = fetch_pairs(keys_low, values_low)
    grad_down = jnp.einsum("tf,td->fd", hidden_low, cotangent, preferred_element_type=jnp.float32)
    d_hidden = jnp.einsum("td,fd->tf", cotangent, shrink_matrix, preferred_element_type=jnp.float32)
    d_gate_up = hidden_back(d_hidden)[0].astype(jnp.bfloat16)
    grad_expand = jnp.einsum(
        "td,tf->df", normed_two_low, d_gate_up, preferred_element_type=jnp.float32
    )
    d_normed_two = jnp.einsum(
        "tf,df->td", d_gate_up, expand_matrix, preferred_element_type=jnp.float32
    )
    d_mid_part, grad_gain_two = norm_two_back(d_normed_two)
    d_mid = cotangent.astype(jnp.float32) + d_mid_part
    d_branch = d_mid.astype(jnp.bfloat16)
    grad_mixing_out = jnp.einsum(
        "tq,td->qd", attended_low, d_branch, preferred_element_type=jnp.float32
    )
    d_attended = (
        jnp.einsum("td,qd->tq", d_branch, mixing_out, preferred_element_type=jnp.float32)
        .astype(jnp.bfloat16)
        .reshape(head_layout_dims)
    )
    delta = jnp.sum(d_attended.astype(jnp.float32) * attended_rows, axis=-1).transpose(1, 2, 0)

    def grad_step(d_query, number):
        key_window_part, value_window_part, probs = probs_of(pairs_back, number)
        d_probs = jnp.einsum(
            "tkgd,skd->kgts", d_attended, value_window_part, preferred_element_type=jnp.float32
        )
        d_scores = (probs * (d_probs - delta[..., None])).astype(jnp.bfloat16)
        new_query = (
            d_query
            + jnp.einsum(
                "kgts,skd->tkgd", d_scores, key_window_part, preferred_element_type=jnp.float32
            )
            * scale
        )
        d_keys = (
            jnp.einsum(
                "kgts,tkgd->skd",
                d_scores,
                query_lower_precision,
                preferred_element_type=jnp.float32,
            )
            * scale
        )
        d_values = jnp.einsum(
            "kgts,tkgd->skd",
            probs.astype(jnp.bfloat16),
            d_attended,
            preferred_element_type=jnp.float32,
        )
        return (
            new_query,
            (d_keys.reshape(block_current, key_width), d_values.reshape(block_current, key_width)),
        )

    d_query, key_value_rows = lax.scan(grad_step, jnp.zeros(head_layout_dims, jnp.float32), numbers)
    local_key_gradient = lax.psum_scatter(
        key_value_rows[0].reshape(group, key_width).astype(jnp.bfloat16),
        "seq",
        scatter_dimension=0,
        tiled=True,
    ).astype(jnp.float32)
    d_values_mine = lax.psum_scatter(
        key_value_rows[1].reshape(group, key_width).astype(jnp.bfloat16),
        "seq",
        scatter_dimension=0,
        tiled=True,
    ).astype(jnp.float32)
    d_query_pre = query_unrot(d_query.reshape(token_rows, QUERY_HEADS, HEAD_SIZE))[0]
    prior_key_gradient = unrotated_keys(
        local_key_gradient.reshape(token_rows, KEY_VALUE_HEADS, HEAD_SIZE)
    )[0]
    d_projected = jnp.concatenate([d_query_pre, prior_key_gradient, d_values_mine], axis=1).astype(
        jnp.bfloat16
    )
    grad_mixing_in = jnp.einsum(
        "td,tq->dq", normed_low, d_projected, preferred_element_type=jnp.float32
    )
    d_normed = jnp.einsum("tq,dq->td", d_projected, mixing_in, preferred_element_type=jnp.float32)
    d_input_part, grad_gain_one = norm_back(d_normed)
    d_input = d_mid + d_input_part
    summed_grads = (
        lax.psum_scatter(
            grad_mixing_in.reshape(-1), ("seq", "dp"), scatter_dimension=0, tiled=True
        ),
        lax.psum_scatter(
            grad_mixing_out.reshape(-1), ("seq", "dp"), scatter_dimension=0, tiled=True
        ),
        lax.psum_scatter(grad_expand.reshape(-1), ("seq", "dp"), scatter_dimension=0, tiled=True),
        lax.psum_scatter(grad_down.reshape(-1), ("seq", "dp"), scatter_dimension=0, tiled=True),
    )
    gain_grads = lax.psum(jnp.stack([grad_gain_one, grad_gain_two]), ("seq", "dp"))
    return (
        result,
        d_input,
        summed_grads[0],
        summed_grads[1],
        summed_grads[2],
        summed_grads[3],
        gain_grads,
    )


def solution(mesh):
    return jax.shard_map(
        per_device,
        mesh=mesh,
        in_specs=(
            P(("seq", "dp"), None),
            P(("seq", "dp")),
            P(("seq", "dp")),
            P(("seq", "dp")),
            P(("seq", "dp")),
            P(),
            P("dp", None),
            P(("seq", "dp"), None),
        ),
        out_specs=(
            P(("seq", "dp"), None),
            P(("seq", "dp"), None),
            P(("seq", "dp")),
            P(("seq", "dp")),
            P(("seq", "dp")),
            P(("seq", "dp")),
            P(),
        ),
        check_vma=False,
    )
```

profile of v0, /device:TPU:0, one launch (start us, length us, event | category | flops | bytes accessed | tf_op | source)
XLA Modules:
  0.0 851.1 jit_solution(7512977916440498301)
XLA Ops:
  13.5 57.5 %all-gather.16.cloned.1.call-done = bf16[32,1,17280]{2,1,0:T(2,128)(2,1)} async-done(((bf16[1,1,17280]{2,1,0:T(2,128)(2,1)}), bf16[32,1,17280]{2,1,0:T(2,128)(2,1)}) %all-gather.16.cloned.1.call-update) | async-done | bytes 1105936 | tf_op jit(solution)/shard_map/all_gather | solution.py:69
  71.0 7.7 reduce.1
  85.7 44.1 %all-gather.1 = bf16[32,1,10368]{2,1,0:T(2,128)(2,1)S(1)} all-gather(bf16[1,1,10368]{2,1,0:T(2,128)(2,1)S(1)} %reshape.464), channel_id=1, replica_groups=mesh['seq'=8,'dp'=4] {'seq','dp'}, dimensions={0}, use_global_device_ids=true | all-gather | bytes 684288 | tf_op jit(solution)/shard_map/all_gather | solution.py:70
  129.7 4.8 reduce.2
  137.6 4.3 reshape.447
  141.9 35.2 %all-gather.10.cloned.1.call-done = bf16[4096,192]{0,1:T(8,128)(2,1)} async-done(((bf16[512,192]{0,1:T(8,128)(2,1)}), bf16[4096,192]{0,1:T(8,128)(2,1)}) %all-gather.10.cloned.1.call-update) | async-done | bytes 1572880 | tf_op jit(solution)/shard_map/all_gather | solution.py:83
  177.1 52.4 %while.42 = (s32[]{:T(128)}, f32[3,3,512]{2,1,0:T(4,128)S(1)}, f32[3,3,512]{2,1,0:T(4,128)S(1)}, s32[512]{0:T(512)S(1)}, s32[8]{0:T(128)S(1)}, /*index=5*/s32[40...) while((s32[]{:T(128)}, f32[3,3,512]{2,1,0:T(4,128)S(1)}, ...), condition=%wide.region_8.9_spmd.clone, body=%wide.region_5.8_spmd.clone.sunk | while | flops 321674240 | bytes 21098720 | solution.py:159
  229.6 65.2 %while.43 = (s32[]{:T(128)}, f32[512,3,3,64]{0,3,2,1:T(8,128)}, s32[8]{0:T(128)S(1)}, bf16[4096,192]{0,1:T(8,128)(2,1)}, s32[512]{0:T(512)S(1)}, /*index=5*/s32[...) while((s32[]{:T(128)}, f32[512,3,3,64]{0,3,2,1:T(8,128)}, ...), condition=%wide.region_10.11_spmd.clone, body=%wide.region_9.10_spmd.clone.sunk | while | flops 617153024 | bytes 4690153 | solution.py:186
  232.4 4.3 fusion.134
  239.4 5.6 fusion.134
  247.7 5.6 fusion.134
  256.0 5.6 fusion.134
  264.3 5.6 fusion.134
  272.6 5.6 fusion.134
  280.9 5.6 fusion.134
  289.2 5.6 fusion.134
  297.0 6.8 reshape.446
  303.8 4.9 fusion.71
  308.8 3.6 fusion.56
  319.7 127.4 %while.44 = (s32[]{:T(128)}, f32[512,3,3,64]{0,3,2,1:T(8,128)S(1)}, bf16[8,512,192]{1,2,0:T(8,128)(2,1)}, bf16[8,512,192]{1,2,0:T(8,128)(2,1)}, s32[8]{0:T(128)S...) while((s32[]{:T(128)}, f32[512,3,3,64]{0,3,2,1:T(8,128)S(1)}, ...), condition=%wide.region_15.16_spmd.clone, body=%wide.region_14.15_spmd.clone.sunk | while | flops 1540129280 | bytes 53109092 | solution.py:254
  329.1 3.5 fusion.146
  408.5 3.5 fusion.146
  452.8 5.0 convolution_bitcast_fusion.1
  457.8 4.5 copy.55
  467.2 4.9 fusion.73
  472.0 5.3 reshape.457
  477.7 35.9 %reduce-scatter.3.cloned.1.call-done = bf16[512,192]{0,1:T(8,128)(2,1)} async-done(((bf16[4096,192]{0,1:T(8,128)(2,1)}), bf16[512,192]{0,1:T(8,128)(2,1)}) %reduce-scatter.3.cloned.1.call-update) | async-done | bytes 196624 | tf_op jit(solution)/shard_map/reduce_scatter | solution.py:255
  514.7 67.1 %reduce-scatter.5.cloned.1.call-done = bf16[512,192]{0,1:T(8,128)(2,1)} async-done(((bf16[4096,192]{0,1:T(8,128)(2,1)}), bf16[512,192]{0,1:T(8,128)(2,1)}) %reduce-scatter.5.cloned.1.call-update) | async-done | bytes 196624 | tf_op jit(solution)/shard_map/reduce_scatter | solution.py:261
  585.0 3.6 reshape.454
  589.4 4.1 fusion.46
  594.5 42.0 %psum.7 = f32[2,576]{1,0:T(2,128)} all-reduce(f32[2,576]{1,0:T(2,128)S(1)} %pad_maximum_fusion.5), channel_id=1, replica_groups=mesh['seq'=8,'dp'=4] {'seq','dp'}, use_global_device_ids=true, to_apply=%region_25.26 | all-reduce | flops 1152 | bytes 9216 | tf_op jit(solution)/shard_map/psum | solution.py:290
  637.9 199.9 %all-reduce.13.cloned.1.call-done = (f32[552960]{0:T(1024)}, f32[331776]{0:T(1024)}, f32[1769472]{0:T(1024)}, f32[884736]{0:T(1024)}) async-done(((f32[552960]{0:T(1024)}, f32[331776]{0:T(1024)}, f32[1769472]{0:T(1024)}, f32[884736]{0:T(1024)}), (f32[552960]{0:T(1024)}, f32[331776]{0:T(1024)}, f32[1769472]{0:T(1024)}, f32[884736]{0:T(1024)})) %all-reduce.13.cloned.1.call-update) | async-done | bytes 14155792
  (446 shorter events, 227.3 us)
Async XLA Ops:
  7.2 63.8 %all-gather.16.cloned.1.call-start = ((), (), s32[]{:S(2)}) async-start(), calls=%async_computation.8 | async-start | bytes 2280960 | tf_op jit(solution)/shard_map/all_gather | solution.py:69
  8.7 128.9 %all-gather.14.cloned.1.call-start = ((), (), s32[]{:S(2)}) async-start(), calls=%async_computation.5 | async-start | bytes 1824768 | tf_op jit(solution)/shard_map/all_gather | solution.py:72
  9.4 167.7 %all-gather.10.cloned.1.call-start = ((), (), s32[]{:S(2)}) async-start(), calls=%async_computation.3 | async-start | bytes 1769472 | tf_op jit(solution)/shard_map/all_gather | solution.py:83
  11.1 68.7 %copy-start.29 = (f32[576]{0:T(1024)}, f32[576]{0:T(1024)S(1)}, u32[]{:S(2)}) copy-start(f32[576]{0:T(1024)S(1)} %get-tuple-element.478) | copy-start | bytes 6916
  13.1 65.6 %copy-start.37 = (f32[512]{0:T(512)}, f32[512]{0:T(512)S(1)}, u32[]{:S(2)}) copy-start(f32[512]{0:T(512)S(1)} %fusion.51) | copy-start | bytes 6148
  13.1 66.7 %copy-start.35 = (f32[512]{0:T(512)}, f32[512]{0:T(512)S(1)}, u32[]{:S(2)}) copy-start(f32[512]{0:T(512)S(1)} %fusion.65) | copy-start | bytes 6148
  13.4 123.9 %copy-start.20 = (f32[512,32]{0,1:T(8,128)}, f32[512,32]{0,1:T(8,128)S(1)}, u32[]{:S(2)}) copy-start(f32[512,32]{0,1:T(8,128)S(1)} %get-tuple-element.574) | copy-start | bytes 196612
  13.5 123.9 %copy-start.22 = (f32[512,32]{0,1:T(8,128)}, f32[512,32]{0,1:T(8,128)S(1)}, u32[]{:S(2)}) copy-start(f32[512,32]{0,1:T(8,128)S(1)} %get-tuple-element.575) | copy-start | bytes 196612
  82.2 3.4 copy-start.34
  83.0 146.6 %all-gather.8.cloned.1.call-start = ((), (), s32[]{:S(2)}) async-start(), calls=%async_computation.2 | async-start | bytes 1769472 | tf_op jit(solution)/shard_map/all_gather | solution.py:84
  84.8 212.2 %all-gather.12.cloned.1.call-start = ((), (), s32[]{:S(2)}) async-start(), calls=%async_computation.4 | async-start | bytes 3649536 | tf_op jit(solution)/shard_map/all_gather | solution.py:71
  85.4 428.2 %reduce-scatter.3.cloned.1.call-start = ((), (), s32[]{:S(2)}) async-start(), calls=%async_computation.6 | async-start | bytes 1769472 | tf_op jit(solution)/shard_map/reduce_scatter | solution.py:255
  303.8 5.0 copy-start.15
  303.8 5.0 copy-start.19
  308.8 3.6 copy-start.3
  449.9 131.9 %reduce-scatter.5.cloned.1.call-start = ((), (), s32[]{:S(2)}) async-start(), calls=%async_computation.7 | async-start | bytes 1769472 | tf_op jit(solution)/shard_map/reduce_scatter | solution.py:261
  452.7 385.0 %all-reduce.13.cloned.1.call-start = ((), (), s32[]{:S(2)}) async-start(), calls=%async_computation.9 | async-start | bytes 28311552
  457.8 4.5 copy-start.1
  457.8 4.5 copy-start.9
  464.1 3.0 copy-start.16
  472.0 5.3 copy-start.21
  472.0 5.3 copy-start.23
  477.6 104.2 %copy-start.30 = (f32[576]{0:T(1024)S(1)}, f32[576]{0:T(1024)}, u32[]{:S(2)}) copy-start(f32[576]{0:T(1024)} %copy-done.29) | copy-start | bytes 6916
  477.6 104.2 %copy-start.36 = (f32[512]{0:T(512)S(1)}, f32[512]{0:T(512)}, u32[]{:S(2)}) copy-start(f32[512]{0:T(512)} %copy-done.35) | copy-start | bytes 6148
  477.7 107.3 %copy-start.24 = (bf16[512,9,64]{0,2,1:T(8,128)(2,1)}, bf16[512,9,64]{0,2,1:T(8,128)(2,1)S(1)}, u32[]{:S(2)}) copy-start(bf16[512,9,64]{0,2,1:T(8,128)(2,1)S(1)} %add_convert_fusion.1) | copy-start | bytes 1769476
  514.6 70.4 %copy-start.26 = (bf16[512,3,64]{0,2,1:T(8,128)(2,1)}, bf16[512,3,64]{0,2,1:T(8,128)(2,1)S(1)}, u32[]{:S(2)}) copy-start(bf16[512,3,64]{0,2,1:T(8,128)(2,1)S(1)} %add_convert_fusion.5) | copy-start | bytes 589828
  589.3 4.1 copy-start.12
  589.3 4.1 copy-start.25
  589.3 4.1 copy-start.27
  589.3 4.1 copy-start.40
  593.5 43.0 %copy-start.38 = (f32[512]{0:T(512)S(1)}, f32[512]{0:T(512)}, u32[]{:S(2)}) copy-start(f32[512]{0:T(512)} %copy-done.37) | copy-start | bytes 6148
  593.5 43.0 %copy-start.2 = (f32[512,576]{0,1:T(8,128)S(1)}, f32[512,576]{0,1:T(8,128)}, u32[]{:S(2)}) copy-start(f32[512,576]{0,1:T(8,128)} %copy-done) | copy-start | bytes 3538948
  (39 other events, 69.7 us)
Sparse Core Ops, SparseCore 0:
  11.4 59.5 all-gather.15
  73.8 55.1 all-gather.13
  131.6 45.3 all-gather.9
  179.6 43.4 all-gather.7
  225.8 58.3 all-gather.11
  450.0 63.5 reduce-scatter.2
  517.4 64.3 reduce-scatter.4
  588.8 248.9 all-reduce.12
where the time goes:
time: 861 us; the launch traced here: 851 us
  waiting for transfers between devices  397 us (46%)
  matrix products  169 us (20%)
  local copies, waits for them, and re-layouts  119 us (14%)
  blocking collectives  86.1 us (10%)
  other arithmetic  47.2 us (5%)
  loops' own time  17.6 us (2%)
  between operations  14.9 us (2%)
    unnamed x9, waiting for transfers between devices  201 us
    reduce_scatter x1, waiting for transfers between devices, per_device(): lax.psum_scatter(key_value_rows[1].reshape(group, key_width).astype(jnp.b...  67.1 us
    all_gather x1, waiting for transfers between devices, fetch_weights(): lax.all_gather(w_qkv, ('seq', 'dp'), axis=0, tiled=True)  57.5 us
    all_gather x1, blocking collectives, fetch_weights(): lax.all_gather(w_out, ('seq', 'dp'), axis=0, tiled=True)  44.1 us
    dot_general x8, matrix products, out_step(): jnp.einsum('kgts,skd->tkgd', probs.astype(jnp.bfloat16), value_window_par...  43.2 us
    psum x1, blocking collectives, per_device(): lax.psum(jnp.stack([grad_gain_one, grad_gain_two]), ('seq', 'dp'))  42 us
    reduce_scatter x1, waiting for transfers between devices, per_device(): lax.psum_scatter(key_value_rows[0].reshape(group, key_width).astype(jnp.b...  35.9 us
    all_gather x1, waiting for transfers between devices, fetch_pairs(): lax.all_gather(keys_mine, 'seq', axis=0, tiled=True)  35.2 us
  transfers between devices with their start and end apart: 8, of which 5 were waited for; matrix products, arithmetic and copies ran while one was open for 20% of the time, Pallas kernels for 0%

commit v1 on v0

--- a/solution.py
+++ b/solution.py
@@ -12,6 +12,18 @@
 EPS = 1e-05
 THETA = 100000.0
 MASKED = -1e30
+
+
+def gather_by_bits(x, axis, dim):
+    ways, here, turn = (lax.axis_size(axis), lax.axis_index(axis), x.shape[dim])
+    line, have = (x, 1)
+    while have < ways:
+        line = jnp.concatenate(
+            [line, lax.ppermute(line, axis, [(d, (d - have) % ways) for d in range(ways)])],
+            axis=dim,
+        )
+        have = 2 * have
+    return jnp.roll(line, here * turn, axis=dim)
 
 
 def rms_norm(value_rows, gain):
@@ -66,7 +78,7 @@
 
     def fetch_weights():
         parts = (
-            lax.all_gather(w_qkv, ("seq", "dp"), axis=0, tiled=True),
+            gather_by_bits(w_qkv, ("seq", "dp"), 0),
             lax.all_gather(w_out, ("seq", "dp"), axis=0, tiled=True),
             lax.all_gather(w_gu, ("seq", "dp"), axis=0, tiled=True),
             lax.all_gather(w_down, ("seq", "dp"), axis=0, tiled=True),

time: 861 us -> 824 us (0.957)
  waiting for transfers between devices: 397 us -> 336 us
  starting transfers between devices: 0.32 us -> 11.2 us
    all_gather x1 -> x0, waiting for transfers between devices: 57.5 us -> none  [fetch_weights(): lax.all_gather(w_qkv, ('seq', 'dp'), axis=0, tiled=True)]
    ppermute x0 -> x5, waiting for transfers between devices: none -> 35.9 us  [gather_by_bits(): lax.ppermute(line, axis, [(d, (d - have) % ways) for d in range(ways)])]
    all_gather x1, waiting for transfers between devices: 35.2 us -> 0.01 us  [fetch_pairs(): lax.all_gather(keys_mine, 'seq', axis=0, tiled=True)]
    ppermute x0 -> x5, starting transfers between devices: none -> 10.9 us  [gather_by_bits(): lax.ppermute(line, axis, [(d, (d - have) % ways) for d in range(ways)])]
    unnamed x83 -> x94, local copies, waits for them, and re-layouts: 16.4 us -> 21.5 us
    unnamed x9 -> x8, waiting for transfers between devices: 201 us -> 201 us
  transfers between devices with their start and end apart: 8 -> 12, of which waited for: 5 -> 8; matrix products, arithmetic and copies ran while one was open for 20% -> 22% of each run, Pallas kernels for 0% -> 0%
where the time goes in v1:
time: 824 us; the launch traced here: 814 us
  waiting for transfers between devices  336 us (41%)
  matrix products  170 us (21%)
  local copies, waits for them, and re-layouts  123 us (15%)
  blocking collectives  93.1 us (11%)
  other arithmetic  47.8 us (6%)
  loops' own time  17.3 us (2%)
  between operations  15.1 us (2%)
  starting transfers between devices  11.2 us (1%)
    unnamed x8, waiting for transfers between devices  201 us
    reduce_scatter x1, waiting for transfers between devices, per_device(): lax.psum_scatter(key_value_rows[1].reshape(group, key_width).astype(jnp.b...  67 us
    all_gather x1, blocking collectives, fetch_weights(): lax.all_gather(w_out, ('seq', 'dp'), axis=0, tiled=True)  51.2 us
    dot_general x8, matrix products, out_step(): jnp.einsum('kgts,skd->tkgd', probs.astype(jnp.bfloat16), value_window_par...  43.2 us
    psum x1, blocking collectives, per_device(): lax.psum(jnp.stack([grad_gain_one, grad_gain_two]), ('seq', 'dp'))  41.9 us
    ppermute x5, waiting for transfers between devices, gather_by_bits(): lax.ppermute(line, axis, [(d, (d - have) % ways) for d in range(ways)])  35.9 us
    reduce_scatter x1, waiting for transfers between devices, per_device(): lax.psum_scatter(key_value_rows[0].reshape(group, key_width).astype(jnp.b...  32.3 us
    dot_general x8, matrix products, grad_step(): jnp.einsum('tkgd,skd->kgts', d_attended, value_window_part, preferred_ele...  27.9 us
  transfers between devices with their start and end apart: 12, of which 8 were waited for; matrix products, arithmetic and copies ran while one was open for 22% of the time, Pallas kernels for 0%

profile of v1, /device:TPU:0, one launch (start us, length us, event | category | flops | bytes accessed | tf_op | source)
XLA Modules:
  0.0 813.7 jit_solution(16531481890212036759)
XLA Ops:
  8.0 6.4 collective-permute-start
  39.2 28.4 %collective-permute-done.4 = bf16[276480]{0:T(1024)(128)(2,1)S(1)} collective-permute-done((bf16[276480]{0:T(1024)(128)(2,1)S(1)}, bf16[276480]{0:T(1024)(128)(2,1)S(1)}, u32[]{:S(2)}, u32[]{:S(2)}) %collective-permute-start.4) | collective-permute-done | bytes 552992 | tf_op jit(solution)/shard_map/ppermute | solution.py:22
  67.7 4.2 fusion.53
  78.6 51.2 %all-gather = bf16[32,1,10368]{2,1,0:T(2,128)(2,1)S(1)} all-gather(bf16[1,1,10368]{2,1,0:T(2,128)(2,1)S(1)} %reshape.462), channel_id=1, replica_groups=mesh['seq'=8,'dp'=4] {'seq','dp'}, dimensions={0}, use_global_device_ids=true | all-gather | bytes 684288 | tf_op jit(solution)/shard_map/all_gather | solution.py:82
  129.9 4.8 reduce.1
  137.7 4.3 reshape.447
  142.1 52.5 %while.42 = (s32[]{:T(128)}, f32[3,3,512]{2,1,0:T(4,128)S(1)}, f32[3,3,512]{2,1,0:T(4,128)S(1)}, s32[512]{0:T(512)S(1)}, s32[8]{0:T(128)S(1)}, /*index=5*/s32[40...) while((s32[]{:T(128)}, f32[3,3,512]{2,1,0:T(4,128)S(1)}, ...), condition=%wide.region_8.10_spmd.clone, body=%wide.region_5.9_spmd.clone.sunk | while | flops 321674240 | bytes 21098720 | solution.py:171
  194.6 65.4 %while.43 = (s32[]{:T(128)}, f32[512,3,3,64]{0,3,2,1:T(8,128)}, s32[8]{0:T(128)S(1)}, bf16[4096,192]{0,1:T(8,128)(2,1)}, s32[512]{0:T(512)S(1)}, /*index=5*/s32[...) while((s32[]{:T(128)}, f32[512,3,3,64]{0,3,2,1:T(8,128)}, ...), condition=%wide.region_10.12_spmd.clone, body=%wide.region_9.11_spmd.clone.sunk | while | flops 617153024 | bytes 4690153 | solution.py:198
  197.4 4.3 fusion.135
  204.4 5.6 fusion.135
  212.7 5.6 fusion.135
  221.2 5.6 fusion.135
  229.5 5.6 fusion.135
  237.8 5.6 fusion.135
  246.1 5.6 fusion.135
  254.4 5.6 fusion.135
  262.3 6.8 reshape.446
  269.1 5.0 fusion.72
  274.0 3.6 fusion.57
  285.0 127.2 %while.44 = (s32[]{:T(128)}, f32[512,3,3,64]{0,3,2,1:T(8,128)S(1)}, bf16[8,512,192]{1,2,0:T(8,128)(2,1)}, bf16[8,512,192]{1,2,0:T(8,128)(2,1)}, s32[8]{0:T(128)S...) while((s32[]{:T(128)}, f32[512,3,3,64]{0,3,2,1:T(8,128)S(1)}, ...), condition=%wide.region_15.17_spmd.clone, body=%wide.region_14.16_spmd.clone.sunk | while | flops 1540129280 | bytes 53109092 | solution.py:266
  294.4 3.5 fusion.147
  310.2 3.5 fusion.147
  417.8 4.9 convolution_bitcast_fusion.1
  422.8 4.4 copy.55
  432.1 4.9 fusion.74
  437.0 5.3 reshape.457
  444.3 32.3 %reduce-scatter.3.cloned.1.call-done = bf16[512,192]{0,1:T(8,128)(2,1)} async-done(((bf16[4096,192]{0,1:T(8,128)(2,1)}), bf16[512,192]{0,1:T(8,128)(2,1)}) %reduce-scatter.3.cloned.1.call-update) | async-done | bytes 196624 | tf_op jit(solution)/shard_map/reduce_scatter | solution.py:267
  477.7 67.0 %reduce-scatter.5.cloned.1.call-done = bf16[512,192]{0,1:T(8,128)(2,1)} async-done(((bf16[4096,192]{0,1:T(8,128)(2,1)}), bf16[512,192]{0,1:T(8,128)(2,1)}) %reduce-scatter.5.cloned.1.call-update) | async-done | bytes 196624 | tf_op jit(solution)/shard_map/reduce_scatter | solution.py:273
  547.9 3.6 reshape.454
  552.9 3.6 fusion.46
  557.6 41.9 %psum.7 = f32[2,576]{1,0:T(2,128)} all-reduce(f32[2,576]{1,0:T(2,128)S(1)} %pad_maximum_fusion.8), channel_id=1, replica_groups=mesh['seq'=8,'dp'=4] {'seq','dp'}, use_global_device_ids=true, to_apply=%region_25.27 | all-reduce | flops 1152 | bytes 9216 | tf_op jit(solution)/shard_map/psum | solution.py:302
  600.9 199.5 %all-reduce.13.cloned.1.call-done = (f32[552960]{0:T(1024)}, f32[331776]{0:T(1024)}, f32[1769472]{0:T(1024)}, f32[884736]{0:T(1024)}) async-done(((f32[552960]{0:T(1024)}, f32[331776]{0:T(1024)}, f32[1769472]{0:T(1024)}, f32[884736]{0:T(1024)}), (f32[552960]{0:T(1024)}, f32[331776]{0:T(1024)}, f32[1769472]{0:T(1024)}, f32[884736]{0:T(1024)})) %all-reduce.13.cloned.1.call-update) | async-done | bytes 14155792
  (471 shorter events, 249.0 us)
Async XLA Ops:
  7.2 23.2 %copy-start.24 = (bf16[17280]{0:T(1024)(128)(2,1)S(1)}, bf16[17280]{0:T(1024)(128)(2,1)}, u32[]{:S(2)}) copy-start(bf16[17280]{0:T(1024)(128)(2,1)} %param.17) | copy-start | bytes 103684
  7.2 23.1 %copy-start.40 = (f32[2,576]{1,0:T(2,128)S(1)}, f32[2,576]{1,0:T(2,128)}, u32[]{:S(2)}) copy-start(f32[2,576]{1,0:T(2,128)} %param.21) | copy-start | bytes 13828
  7.2 130.5 %all-gather.12.cloned.1.call-start = ((), (), s32[]{:S(2)}) async-start(), calls=%async_computation.5 | async-start | bytes 1824768 | tf_op jit(solution)/shard_map/all_gather | solution.py:84
  7.9 134.1 %all-gather.8.cloned.1.call-start = ((), (), s32[]{:S(2)}) async-start(), calls=%async_computation.3 | async-start | bytes 1769472 | tf_op jit(solution)/shard_map/all_gather | solution.py:95
  8.0 8.4 %collective-permute-start = (bf16[17280]{0:T(1024)(128)(2,1)}, bf16[17280]{0:T(1024)(128)(2,1)S(1)}, u32[]{:S(2)}, u32[]{:S(2)}) collective-permute-start(bf16[17280]{0:T(1024)(128)(2,1)} %param.17), channel_id=1, source_target_pairs={{0,31},{1,0},{2,1},{3,2},{4,3},{5,4},{6,5},{7,6},{8,7},{9,8},{10,9... | collective-permute-start | bytes 103688 | tf_op jit(solution)/shard_map/ppermute | solution.py:22
  17.1 4.4 collective-permute-start.1
  22.3 5.1 collective-permute-start.2
  24.1 43.6 %copy-start.38 = (f32[512]{0:T(512)}, f32[512]{0:T(512)S(1)}, u32[]{:S(2)}) copy-start(f32[512]{0:T(512)S(1)} %fusion.51) | copy-start | bytes 6148
  28.2 9.4 %collective-permute-start.3 = (bf16[138240]{0:T(1024)(128)(2,1)S(1)}, bf16[138240]{0:T(1024)(128)(2,1)S(1)}, u32[]{:S(2)}, u32[]{:S(2)}) collective-permute-start(bf16[138240]{0:T(1024)(128)(2,1)S(1)} %pad_maximum_fusion.4), channel_id=1, source_target_pairs={{0,24},{1,25},{2,26},{3,27},{4,28},{5,29},{6,30},{7,31},{8,0},{9,1... | collective-permute-start | bytes 829448 | tf_op jit(solution)/shard_map/ppermute | solution.py:22
  30.3 43.4 %copy-start.30 = (f32[576]{0:T(1024)}, f32[576]{0:T(1024)S(1)}, u32[]{:S(2)}) copy-start(f32[576]{0:T(1024)S(1)} %get-tuple-element.479) | copy-start | bytes 6916
  31.6 42.1 %copy-start.36 = (f32[512]{0:T(512)}, f32[512]{0:T(512)S(1)}, u32[]{:S(2)}) copy-start(f32[512]{0:T(512)S(1)} %fusion.66) | copy-start | bytes 6148
  37.6 30.0 %collective-permute-start.4 = (bf16[276480]{0:T(1024)(128)(2,1)S(1)}, bf16[276480]{0:T(1024)(128)(2,1)S(1)}, u32[]{:S(2)}, u32[]{:S(2)}) collective-permute-start(bf16[276480]{0:T(1024)(128)(2,1)S(1)} %get-tuple-element.575), channel_id=1, source_target_pairs={{0,16},{1,17},{2,18},{3,19},{4,20},{5,21},{6,22},{7,23},{8,24},{9,... | collective-permute-start | bytes 1658888 | tf_op jit(solution)/shard_map/ppermute | solution.py:22
  39.2 98.3 %copy-start.20 = (f32[512,32]{0,1:T(8,128)}, f32[512,32]{0,1:T(8,128)S(1)}, u32[]{:S(2)}) copy-start(f32[512,32]{0,1:T(8,128)S(1)} %get-tuple-element.577) | copy-start | bytes 196612
  39.2 98.2 %copy-start.22 = (f32[512,32]{0,1:T(8,128)}, f32[512,32]{0,1:T(8,128)S(1)}, u32[]{:S(2)}) copy-start(f32[512,32]{0,1:T(8,128)S(1)} %get-tuple-element.578) | copy-start | bytes 196612
  77.0 117.6 %all-gather.6.cloned.1.call-start = ((), (), s32[]{:S(2)}) async-start(), calls=%async_computation.2 | async-start | bytes 1769472 | tf_op jit(solution)/shard_map/all_gather | solution.py:96
  77.8 184.5 %all-gather.10.cloned.1.call-start = ((), (), s32[]{:S(2)}) async-start(), calls=%async_computation.4 | async-start | bytes 3649536 | tf_op jit(solution)/shard_map/all_gather | solution.py:83
  78.4 398.2 %reduce-scatter.3.cloned.1.call-start = ((), (), s32[]{:S(2)}) async-start(), calls=%async_computation.6 | async-start | bytes 1769472 | tf_op jit(solution)/shard_map/reduce_scatter | solution.py:267
  269.0 5.0 copy-start.15
  269.0 5.0 copy-start.19
  414.9 129.7 %reduce-scatter.5.cloned.1.call-start = ((), (), s32[]{:S(2)}) async-start(), calls=%async_computation.7 | async-start | bytes 1769472 | tf_op jit(solution)/shard_map/reduce_scatter | solution.py:273
  417.8 382.6 %all-reduce.13.cloned.1.call-start = ((), (), s32[]{:S(2)}) async-start(), calls=%async_computation.8 | async-start | bytes 28311552
  422.8 4.5 copy-start.1
  422.8 4.5 copy-start.9
  443.4 34.2 %copy-start.21 = (f32[512,32]{0,1:T(8,128)S(1)}, f32[512,32]{0,1:T(8,128)}, u32[]{:S(2)}) copy-start(f32[512,32]{0,1:T(8,128)} %copy-done.20) | copy-start | bytes 196612
  443.4 34.2 %copy-start.23 = (f32[512,32]{0,1:T(8,128)S(1)}, f32[512,32]{0,1:T(8,128)}, u32[]{:S(2)}) copy-start(f32[512,32]{0,1:T(8,128)} %copy-done.22) | copy-start | bytes 196612
  443.4 101.3 %copy-start.31 = (f32[576]{0:T(1024)S(1)}, f32[576]{0:T(1024)}, u32[]{:S(2)}) copy-start(f32[576]{0:T(1024)} %copy-done.30) | copy-start | bytes 6916
  443.4 101.3 %copy-start.37 = (f32[512]{0:T(512)S(1)}, f32[512]{0:T(512)}, u32[]{:S(2)}) copy-start(f32[512]{0:T(512)} %copy-done.36) | copy-start | bytes 6148
  444.3 100.4 %copy-start.25 = (bf16[512,9,64]{0,2,1:T(8,128)(2,1)S(1)}, bf16[512,9,64]{0,2,1:T(8,128)(2,1)}, u32[]{:S(2)}) copy-start(bf16[512,9,64]{0,2,1:T(8,128)(2,1)} %add_convert_fusion.1) | copy-start | bytes 1769476
  477.7 70.2 %copy-start.27 = (bf16[512,3,64]{0,2,1:T(8,128)(2,1)}, bf16[512,3,64]{0,2,1:T(8,128)(2,1)S(1)}, u32[]{:S(2)}) copy-start(bf16[512,3,64]{0,2,1:T(8,128)(2,1)S(1)} %add_convert_fusion.5) | copy-start | bytes 589828
  552.9 3.7 copy-start.42
  556.6 42.9 %copy-start.39 = (f32[512]{0:T(512)S(1)}, f32[512]{0:T(512)}, u32[]{:S(2)}) copy-start(f32[512]{0:T(512)} %copy-done.38) | copy-start | bytes 6148
  556.6 42.9 %copy-start.2 = (f32[512,576]{0,1:T(8,128)S(1)}, f32[512,576]{0,1:T(8,128)}, u32[]{:S(2)}) copy-start(f32[512,576]{0,1:T(8,128)} %copy-done) | copy-start | bytes 3538948
  (45 other events, 92.1 us)
Sparse Core Ops, SparseCore 0:
  10.9 69.6 all-gather.11
  83.1 47.0 all-gather.7
  132.9 43.8 all-gather.5
  179.5 58.5 all-gather.9
  415.1 61.4 reduce-scatter.2
  480.3 64.3 reduce-scatter.4
  551.6 248.7 all-reduce.12
